TPU v7x, 32 devices: a whole 2x2x4 slice. The times are simulated.
32 devices in a mesh: seq: 4 (over y, x), dp: 8 (over z, core).
Axes of the slice: x: 2, y: 2, z: 4, core: 2. Of those that a mesh axis runs over, the one named last changes fastest.
Arguments:
- frames: bfloat16 [16, 512, 3072], P('dp', 'seq'), may hold values from -6 to 6
- proj_weight: bfloat16 [3072, 4608], P('dp'), may hold values from -0.109375 to 0.109375
- rate_weight: bfloat16 [3072, 24], replicated, may hold values from -0.109375 to 0.109375
- rate_bias: float32 [24], replicated, may hold values from -2 to 1
- init_weights: float32 [2, 24, 64, 256], replicated, may hold values from -0.75 to 0.75
- init_bias_hidden: float32 [24, 256], replicated, may hold values from -3 to 3
- init_bias_out: float32 [24, 64], replicated, may hold values from -3 to 3
- out_gain: float32 [1536], replicated, may hold values from 0.5 to 1.5
Outputs:
- ttt_output: bfloat16 [16, 512, 1536], P('dp', 'seq')
All inputs are finite; a program needn't handle non-finite values.
Results may differ from a plain program's by a relative error of at most 0.0091.
Values may be sent and summed in bfloat16 or wider, within the bound.
A program may use at most 128 MiB of HBM per device.

v0:
```python
import math

import jax
import jax.numpy as jnp
from jax import lax
from jax.sharding import PartitionSpec as P

MB = 64


precise = lax.Precision.HIGHEST
coefficient = 0.044715
root_scale = math.sqrt(2.0 / math.pi)


def shortened(x):
    return jax.tree.map(lambda a: a.astype(jnp.bfloat16) if a.dtype == jnp.float32 else a, x)


def shifted(block, axis, distance):
    devices = range(lax.axis_size(axis))
    route = [(i - distance, i) for i in devices if i - distance in devices]
    return lax.ppermute(block, axis, route)


def gelu_pair(z_value):
    tanh_part = jnp.tanh(root_scale * (z_value + coefficient * z_value * z_value * z_value))
    result = 0.5 * z_value * (1.0 + tanh_part)
    derivative = 0.5 * (1.0 + tanh_part) + 0.5 * z_value * (
        1.0 - tanh_part * tanh_part
    ) * root_scale * (1.0 + 3.0 * coefficient * z_value * z_value)
    return (result, derivative)


def minibatch(carried, inputs):
    pair, bias_hidden, bias_out = carried
    queries, key_rows, values, step_rate = inputs
    w_first = pair[0]
    w_second = pair[1]
    block_len = queries.shape[1]
    causal = jnp.tril(jnp.ones((block_len, block_len), dtype=bool))
    z_first = (
        jnp.einsum("hbd,hdf->hbf", key_rows, w_first, precision=precise) + bias_hidden[:, None, :]
    )
    hidden, derivative = gelu_pair(z_first)
    z_second = (
        jnp.einsum("hbf,hdf->hbd", hidden, w_second, precision=precise) + bias_out[:, None, :]
    )
    grad_second = z_second - (values - key_rows)
    grad_first = jnp.einsum("hbd,hdf->hbf", grad_second, w_second, precision=precise) * derivative
    scores_first = jnp.einsum("htd,hsd->hts", queries, key_rows, precision=precise) + 1.0
    mix_first = jnp.where(causal[None], scores_first * step_rate[:, None, :], 0.0)
    zq_first = (
        jnp.einsum("htd,hdf->htf", queries, w_first, precision=precise) + bias_hidden[:, None, :]
    )
    zq_first = zq_first - jnp.einsum("hts,hsf->htf", mix_first, grad_first, precision=precise)
    hidden_query, unused = gelu_pair(zq_first)
    scores_second = jnp.einsum("htf,hsf->hts", hidden_query, hidden, precision=precise) + 1.0
    mix_second = jnp.where(causal[None], scores_second * step_rate[:, None, :], 0.0)
    zq_second = (
        jnp.einsum("htf,hdf->htd", hidden_query, w_second, precision=precise) + bias_out[:, None, :]
    )
    zq_second = zq_second - jnp.einsum("hts,hsd->htd", mix_second, grad_second, precision=precise)
    scaled_first = grad_first * step_rate[:, :, None]
    scaled_second = grad_second * step_rate[:, :, None]
    new_first = w_first - jnp.einsum("hbd,hbf->hdf", key_rows, scaled_first, precision=precise)
    new_second = w_second - jnp.einsum("hbd,hbf->hdf", scaled_second, hidden, precision=precise)
    new_pair = jnp.stack([new_first, new_second])
    new_hidden = bias_hidden - jnp.sum(scaled_first, axis=1)
    new_out = bias_out - jnp.sum(scaled_second, axis=1)
    return ((new_pair, new_hidden, new_out), queries + zq_second)


def run_slab(start_state, column_block, rate_block, gain_rows):
    slab_len = column_block.shape[0]
    group_heads = column_block.shape[2]
    head_size = column_block.shape[3]
    batches = slab_len // MB
    inputs = (
        column_block.astype(jnp.float32)
        .reshape(batches, MB, 3, group_heads, head_size)
        .transpose(2, 0, 3, 1, 4)
    )
    step_rate = rate_block.reshape(batches, MB, group_heads).transpose(0, 2, 1)
    final_state, results = lax.scan(
        minibatch, start_state, (inputs[0], inputs[1], inputs[2], step_rate)
    )
    results = results.transpose(0, 2, 1, 3).reshape(slab_len, group_heads, head_size)
    normed = (
        results * lax.rsqrt(jnp.mean(results * results, axis=-1, keepdims=True) + 1e-06) * gain_rows
    )
    return (final_state, normed.reshape(slab_len, group_heads * head_size).astype(jnp.bfloat16))


def on_device(
    frames,
    proj_weight,
    rate_weight,
    rate_bias,
    init_weights,
    init_bias_hidden,
    init_bias_out,
    out_gain,
):
    clip_count, slab_len, model_width = frames.shape
    head_count = rate_weight.shape[1]
    head_size = init_weights.shape[2]
    inner_width = init_weights.shape[3]
    token_rows = frames.reshape(clip_count * slab_len, model_width)
    full_weight = lax.all_gather(proj_weight, "dp", axis=0, tiled=True)
    projected = jnp.dot(token_rows, full_weight, preferred_element_type=jnp.float32)
    projected = projected.astype(jnp.bfloat16).reshape(
        clip_count, slab_len, 3, head_count, head_size
    )
    rates = jax.nn.sigmoid(
        jnp.dot(token_rows, rate_weight, preferred_element_type=jnp.float32) + rate_bias
    ) / (MB * (head_size + inner_width))
    rates = rates.reshape(clip_count, slab_len, head_count)
    gain_all = out_gain.reshape(head_count, head_size)
    length = lax.axis_size("seq")
    position = lax.axis_index("seq")
    turns = clip_count + length - 1
    received_start = (
        jnp.zeros((2, head_count, head_size, inner_width), jnp.bfloat16),
        jnp.zeros((head_count, inner_width), jnp.bfloat16),
        jnp.zeros((head_count, head_size), jnp.bfloat16),
    )
    outputs_start = jnp.zeros((clip_count, slab_len, head_count * head_size), jnp.bfloat16)
    own_state = (init_weights, init_bias_hidden, init_bias_out)

    def one_turn(turn_index, carry):
        received, outputs = carry
        unit_index = turn_index - position
        active = (unit_index >= 0) & (unit_index < clip_count)
        clip_index = jnp.clip(unit_index, 0, clip_count - 1)
        start_state = jax.tree.map(
            lambda member, other: jnp.where(position == 0, member, other.astype(jnp.float32)),
            own_state,
            received,
        )

        def run_unit(operands):
            entry_state, current = operands
            clip_block = lax.dynamic_index_in_dim(projected, clip_index, 0, keepdims=False)
            rate_block = lax.dynamic_index_in_dim(rates, clip_index, 0, keepdims=False)
            final_state, result = run_slab(entry_state, clip_block, rate_block, gain_all)
            current = lax.dynamic_update_slice(
                current, result[None], (clip_index, jnp.int32(0), jnp.int32(0))
            )
            return (jax.tree.map(lambda member: member.astype(jnp.bfloat16), final_state), current)

        def pass_through(operands):
            entry_state, current = operands
            return (jax.tree.map(lambda member: member.astype(jnp.bfloat16), entry_state), current)

        sent, outputs = lax.cond(active, run_unit, pass_through, (start_state, outputs))
        received = jax.tree.map(
            lambda part, own: part.astype(own.dtype), shifted(shortened(sent), "seq", 1), sent
        )
        return (received, outputs)

    unused, outputs = lax.fori_loop(0, turns, one_turn, (received_start, outputs_start))
    return outputs


def solution(mesh):
    return jax.shard_map(
        on_device,
        mesh=mesh,
        in_specs=(P("dp", "seq", None), P("dp", None), P(), P(), P(), P(), P(), P()),
        out_specs=P("dp", "seq", None),
        check_vma=False,
    )
```

profile of v0, /device:TPU:6, one launch (start us, length us, event | category | flops | bytes accessed | tf_op | source)
XLA Modules:
  0.0 1058.8 jit_solution(17548003720531773729)
XLA Ops:
  8.5 247.4 %all-gather.2.cloned.1.call-done = bf16[3072,4608]{1,0:T(8,128)(2,1)} async-done(((bf16[384,4608]{1,0:T(8,128)(2,1)}), bf16[3072,4608]{1,0:T(8,128)(2,1)}) %all-gather.2.cloned.1.call-update) | async-done | bytes 28311568 | tf_op jit(solution)/shard_map/all_gather | solution.py:110
  255.9 14.3 %convolution_convert_fusion = bf16[256,4608]{1,0:T(8,128)(2,1)} fusion(bf16[256,3072]{1,0:T(8,128)(2,1)S(1)} %bitcast.166, bf16[3072,4608]{1,0:T(8,128)(2,1)} %all-gather.2.cloned.1.call-done), kind=kOutput, calls=%fused_computation.74 | convolution fusion | flops 7248936960 | bytes 32243712 | tf_op jit(solution)/shard_map/dot_general | solution.py:111
  270.2 7.0 reshape.105
  277.2 6.4 copy.44
  286.0 763.6 %while.36 = (s32[]{:T(128)}, bf16[2,24,64,256]{3,2,1,0:T(8,128)(2,1)}, bf16[24,256]{1,0:T(8,128)(2,1)S(1)}, bf16[24,64]{1,0:T(8,128)(2,1)S(1)}, bf16[2,128,1536]...) while((s32[]{:T(128)}, ...), condition=%wide.region_8.9_spmd, body=%wide.region_0.8_spmd.sunk | while | flops 2897933824 | bytes 141774256 | solution.py:162
  293.6 35.1 %collective-permute-done.2 = bf16[24,64]{1,0:T(8,128)(2,1)S(1)} collective-permute-done((bf16[24,64]{1,0:T(8,128)(2,1)S(1)}, bf16[24,64]{1,0:T(8,128)(2,1)S(1)}, u32[]{:S(2)}, u32[]{:S(2)}) %collective-permute-start.2) | collective-permute-done | bytes 3104 | tf_op jit(solution)/shard_map/while/body/eval_jaxpr/ppermute | solution.py:23
  337.4 34.3 %collective-permute-done.2 = bf16[24,64]{1,0:T(8,128)(2,1)S(1)} collective-permute-done((bf16[24,64]{1,0:T(8,128)(2,1)S(1)}, bf16[24,64]{1,0:T(8,128)(2,1)S(1)}, u32[]{:S(2)}, u32[]{:S(2)}) %collective-permute-start.2) | collective-permute-done | bytes 3104 | tf_op jit(solution)/shard_map/while/body/eval_jaxpr/ppermute | solution.py:23
  380.3 363.3 %collective-permute-done.2 = bf16[24,64]{1,0:T(8,128)(2,1)S(1)} collective-permute-done((bf16[24,64]{1,0:T(8,128)(2,1)S(1)}, bf16[24,64]{1,0:T(8,128)(2,1)S(1)}, u32[]{:S(2)}, u32[]{:S(2)}) %collective-permute-start.2) | collective-permute-done | bytes 3104 | tf_op jit(solution)/shard_map/while/body/eval_jaxpr/ppermute | solution.py:23
  747.0 110.5 %conditional.2 = ((bf16[2,128,1536]{1,2,0:T(8,128)(2,1)}, f32[2,24,64,256]{3,2,1,0:T(8,128)S(1)}, f32[24,256]{1,0:T(8,128)S(1)}, f32[24,64]{1,0:T(8,128)S(1)})) conditional(s32[]{:T(128)} %convert_element_type.81, (bf16[2,128,1536]{1,2,0:T(8,128)(2,1)}, f32[2,24,64,256]{3,2,1,0:T(8,128)S(1)}, f32[24,256]{1,0:T(8,128)S(1)}, ...), branch_computations={%region_1.1_spmd, %region_2.7_spmd} | conditional | flops 2895551488 | bytes 116423672 | solution.py:156
  747.0 3.0 dynamic-slice_convert_fusion
  750.1 5.8 reshape.104
  755.9 3.8 slice_bitcast_fusion
  759.8 86.8 %while.35 = (s32[]{:T(128)}, f32[2,24,64,256]{3,2,1,0:T(8,128)S(1)}, f32[24,256]{1,0:T(8,128)S(1)}, f32[24,64]{1,0:T(8,128)S(1)}, f32[2,24,64,64]{3,2,1,0:T(8,12...) while((s32[]{:T(128)}, ...), condition=%wide.region_6.5_spmd, body=%wide.region_3.4_spmd.sunk | while | flops 2893975552 | bytes 98181968 | solution.py:85
  770.7 3.0 copy.61
  773.7 4.1 multiply_reduce_fusion.5
  798.3 4.5 fusion.140
  814.1 3.0 copy.61
  817.1 4.1 multiply_reduce_fusion.5
  841.7 4.5 fusion.140
  846.6 3.7 copy.41
  862.8 34.0 %collective-permute-done.2 = bf16[24,64]{1,0:T(8,128)(2,1)S(1)} collective-permute-done((bf16[24,64]{1,0:T(8,128)(2,1)S(1)}, bf16[24,64]{1,0:T(8,128)(2,1)S(1)}, u32[]{:S(2)}, u32[]{:S(2)}) %collective-permute-start.2) | collective-permute-done | bytes 3104 | tf_op jit(solution)/shard_map/while/body/eval_jaxpr/ppermute | solution.py:23
  900.1 110.5 %conditional.2 = ((bf16[2,128,1536]{1,2,0:T(8,128)(2,1)}, f32[2,24,64,256]{3,2,1,0:T(8,128)S(1)}, f32[24,256]{1,0:T(8,128)S(1)}, f32[24,64]{1,0:T(8,128)S(1)})) conditional(s32[]{:T(128)} %convert_element_type.81, (bf16[2,128,1536]{1,2,0:T(8,128)(2,1)}, f32[2,24,64,256]{3,2,1,0:T(8,128)S(1)}, f32[24,256]{1,0:T(8,128)S(1)}, ...), branch_computations={%region_1.1_spmd, %region_2.7_spmd} | conditional | flops 2895551488 | bytes 116423672 | solution.py:156
  900.1 3.0 dynamic-slice_convert_fusion
  903.1 5.8 reshape.104
  909.0 3.8 slice_bitcast_fusion
  912.9 86.8 %while.35 = (s32[]{:T(128)}, f32[2,24,64,256]{3,2,1,0:T(8,128)S(1)}, f32[24,256]{1,0:T(8,128)S(1)}, f32[24,64]{1,0:T(8,128)S(1)}, f32[2,24,64,64]{3,2,1,0:T(8,12...) while((s32[]{:T(128)}, ...), condition=%wide.region_6.5_spmd, body=%wide.region_3.4_spmd.sunk | while | flops 2893975552 | bytes 98181968 | solution.py:85
  926.8 4.1 multiply_reduce_fusion.5
  951.4 4.5 fusion.140
  970.2 4.1 multiply_reduce_fusion.5
  994.8 4.5 fusion.140
  999.7 3.7 copy.41
  1015.9 32.5 %collective-permute-done.2 = bf16[24,64]{1,0:T(8,128)(2,1)S(1)} collective-permute-done((bf16[24,64]{1,0:T(8,128)(2,1)S(1)}, bf16[24,64]{1,0:T(8,128)(2,1)S(1)}, u32[]{:S(2)}, u32[]{:S(2)}) %collective-permute-start.2) | collective-permute-done | bytes 3104 | tf_op jit(solution)/shard_map/while/body/eval_jaxpr/ppermute | solution.py:23
  (251 shorter events, 196.3 us)
Async XLA Ops:
  6.5 249.3 %all-gather.2.cloned.1.call-start = ((), (), s32[]{:S(2)}) async-start(), calls=%async_computation | async-start | bytes 31850496 | tf_op jit(solution)/shard_map/all_gather | solution.py:110
  289.7 39.1 %collective-permute-start = (bf16[2,24,64,256]{3,2,1,0:T(8,128)(2,1)}, bf16[2,24,64,256]{3,2,1,0:T(8,128)(2,1)S(1)}, u32[]{:S(2)}, u32[]{:S(2)}) collective-permute-start(bf16[2,24,64,256]{3,2,1,0:T(8,128)(2,1)} %convert_element_type.82), channel_id=1, source_target_pairs={{0,8},{8,16},{16,24},{1,9},{9,17},{17,25},{2,10},{10,18},{18,26},{... | collective-permute-start | bytes 4718600 | tf_op jit(solution)/shard_map/while/body/eval_jaxpr/ppermute | solution.py:23
  291.0 37.7 %collective-permute-start.1 = (bf16[24,256]{1,0:T(8,128)(2,1)S(1)}, bf16[24,256]{1,0:T(8,128)(2,1)S(1)}, u32[]{:S(2)}, u32[]{:S(2)}) collective-permute-start(bf16[24,256]{1,0:T(8,128)(2,1)S(1)} %convert_element_type.83), channel_id=1, source_target_pairs={{0,8},{8,16},{16,24},{1,9},{9,17},{17,25},{2,10},{10,18},{18,26},{... | collective-permute-start | bytes 36872 | tf_op jit(solution)/shard_map/while/body/eval_jaxpr/ppermute | solution.py:23
  292.3 36.4 %collective-permute-start.2 = (bf16[24,64]{1,0:T(8,128)(2,1)S(1)}, bf16[24,64]{1,0:T(8,128)(2,1)S(1)}, u32[]{:S(2)}, u32[]{:S(2)}) collective-permute-start(bf16[24,64]{1,0:T(8,128)(2,1)S(1)} %convert_element_type.84), channel_id=1, source_target_pairs={{0,8},{8,16},{16,24},{1,9},{9,17},{17,25},{2,10},{10,18},{18,26},{... | collective-permute-start | bytes 9224 | tf_op jit(solution)/shard_map/while/body/eval_jaxpr/ppermute | solution.py:23
  333.5 38.2 %collective-permute-start = (bf16[2,24,64,256]{3,2,1,0:T(8,128)(2,1)}, bf16[2,24,64,256]{3,2,1,0:T(8,128)(2,1)S(1)}, u32[]{:S(2)}, u32[]{:S(2)}) collective-permute-start(bf16[2,24,64,256]{3,2,1,0:T(8,128)(2,1)} %convert_element_type.82), channel_id=1, source_target_pairs={{0,8},{8,16},{16,24},{1,9},{9,17},{17,25},{2,10},{10,18},{18,26},{... | collective-permute-start | bytes 4718600 | tf_op jit(solution)/shard_map/while/body/eval_jaxpr/ppermute | solution.py:23
  334.8 36.9 %collective-permute-start.1 = (bf16[24,256]{1,0:T(8,128)(2,1)S(1)}, bf16[24,256]{1,0:T(8,128)(2,1)S(1)}, u32[]{:S(2)}, u32[]{:S(2)}) collective-permute-start(bf16[24,256]{1,0:T(8,128)(2,1)S(1)} %convert_element_type.83), channel_id=1, source_target_pairs={{0,8},{8,16},{16,24},{1,9},{9,17},{17,25},{2,10},{10,18},{18,26},{... | collective-permute-start | bytes 36872 | tf_op jit(solution)/shard_map/while/body/eval_jaxpr/ppermute | solution.py:23
  336.1 35.6 %collective-permute-start.2 = (bf16[24,64]{1,0:T(8,128)(2,1)S(1)}, bf16[24,64]{1,0:T(8,128)(2,1)S(1)}, u32[]{:S(2)}, u32[]{:S(2)}) collective-permute-start(bf16[24,64]{1,0:T(8,128)(2,1)S(1)} %convert_element_type.84), channel_id=1, source_target_pairs={{0,8},{8,16},{16,24},{1,9},{9,17},{17,25},{2,10},{10,18},{18,26},{... | collective-permute-start | bytes 9224 | tf_op jit(solution)/shard_map/while/body/eval_jaxpr/ppermute | solution.py:23
  376.4 367.3 %collective-permute-start = (bf16[2,24,64,256]{3,2,1,0:T(8,128)(2,1)}, bf16[2,24,64,256]{3,2,1,0:T(8,128)(2,1)S(1)}, u32[]{:S(2)}, u32[]{:S(2)}) collective-permute-start(bf16[2,24,64,256]{3,2,1,0:T(8,128)(2,1)} %convert_element_type.82), channel_id=1, source_target_pairs={{0,8},{8,16},{16,24},{1,9},{9,17},{17,25},{2,10},{10,18},{18,26},{... | collective-permute-start | bytes 4718600 | tf_op jit(solution)/shard_map/while/body/eval_jaxpr/ppermute | solution.py:23
  377.7 366.0 %collective-permute-start.1 = (bf16[24,256]{1,0:T(8,128)(2,1)S(1)}, bf16[24,256]{1,0:T(8,128)(2,1)S(1)}, u32[]{:S(2)}, u32[]{:S(2)}) collective-permute-start(bf16[24,256]{1,0:T(8,128)(2,1)S(1)} %convert_element_type.83), channel_id=1, source_target_pairs={{0,8},{8,16},{16,24},{1,9},{9,17},{17,25},{2,10},{10,18},{18,26},{... | collective-permute-start | bytes 36872 | tf_op jit(solution)/shard_map/while/body/eval_jaxpr/ppermute | solution.py:23
  379.0 364.7 %collective-permute-start.2 = (bf16[24,64]{1,0:T(8,128)(2,1)S(1)}, bf16[24,64]{1,0:T(8,128)(2,1)S(1)}, u32[]{:S(2)}, u32[]{:S(2)}) collective-permute-start(bf16[24,64]{1,0:T(8,128)(2,1)S(1)} %convert_element_type.84), channel_id=1, source_target_pairs={{0,8},{8,16},{16,24},{1,9},{9,17},{17,25},{2,10},{10,18},{18,26},{... | collective-permute-start | bytes 9224 | tf_op jit(solution)/shard_map/while/body/eval_jaxpr/ppermute | solution.py:23
  762.0 2.8 copy-start.8
  762.1 2.8 copy-start.9
  773.7 4.1 copy-start.4
  798.3 4.5 copy-start.5
  805.4 2.8 copy-start.8
  805.4 2.8 copy-start.9
  817.1 4.1 copy-start.4
  841.7 4.5 copy-start.5
  858.8 38.0 %collective-permute-start = (bf16[2,24,64,256]{3,2,1,0:T(8,128)(2,1)}, bf16[2,24,64,256]{3,2,1,0:T(8,128)(2,1)S(1)}, u32[]{:S(2)}, u32[]{:S(2)}) collective-permute-start(bf16[2,24,64,256]{3,2,1,0:T(8,128)(2,1)} %convert_element_type.82), channel_id=1, source_target_pairs={{0,8},{8,16},{16,24},{1,9},{9,17},{17,25},{2,10},{10,18},{18,26},{... | collective-permute-start | bytes 4718600 | tf_op jit(solution)/shard_map/while/body/eval_jaxpr/ppermute | solution.py:23
  860.1 36.7 %collective-permute-start.1 = (bf16[24,256]{1,0:T(8,128)(2,1)S(1)}, bf16[24,256]{1,0:T(8,128)(2,1)S(1)}, u32[]{:S(2)}, u32[]{:S(2)}) collective-permute-start(bf16[24,256]{1,0:T(8,128)(2,1)S(1)} %convert_element_type.83), channel_id=1, source_target_pairs={{0,8},{8,16},{16,24},{1,9},{9,17},{17,25},{2,10},{10,18},{18,26},{... | collective-permute-start | bytes 36872 | tf_op jit(solution)/shard_map/while/body/eval_jaxpr/ppermute | solution.py:23
  861.5 35.3 %collective-permute-start.2 = (bf16[24,64]{1,0:T(8,128)(2,1)S(1)}, bf16[24,64]{1,0:T(8,128)(2,1)S(1)}, u32[]{:S(2)}, u32[]{:S(2)}) collective-permute-start(bf16[24,64]{1,0:T(8,128)(2,1)S(1)} %convert_element_type.84), channel_id=1, source_target_pairs={{0,8},{8,16},{16,24},{1,9},{9,17},{17,25},{2,10},{10,18},{18,26},{... | collective-permute-start | bytes 9224 | tf_op jit(solution)/shard_map/while/body/eval_jaxpr/ppermute | solution.py:23
  915.1 2.8 copy-start.8
  915.2 2.8 copy-start.9
  926.8 4.1 copy-start.4
  951.4 4.5 copy-start.5
  958.5 2.8 copy-start.8
  958.5 2.8 copy-start.9
  970.2 4.1 copy-start.4
  994.8 4.5 copy-start.5
  1011.9 36.4 %collective-permute-start = (bf16[2,24,64,256]{3,2,1,0:T(8,128)(2,1)}, bf16[2,24,64,256]{3,2,1,0:T(8,128)(2,1)S(1)}, u32[]{:S(2)}, u32[]{:S(2)}) collective-permute-start(bf16[2,24,64,256]{3,2,1,0:T(8,128)(2,1)} %convert_element_type.82), channel_id=1, source_target_pairs={{0,8},{8,16},{16,24},{1,9},{9,17},{17,25},{2,10},{10,18},{18,26},{... | collective-permute-start | bytes 4718600 | tf_op jit(solution)/shard_map/while/body/eval_jaxpr/ppermute | solution.py:23
  1013.2 35.1 %collective-permute-start.1 = (bf16[24,256]{1,0:T(8,128)(2,1)S(1)}, bf16[24,256]{1,0:T(8,128)(2,1)S(1)}, u32[]{:S(2)}, u32[]{:S(2)}) collective-permute-start(bf16[24,256]{1,0:T(8,128)(2,1)S(1)} %convert_element_type.83), channel_id=1, source_target_pairs={{0,8},{8,16},{16,24},{1,9},{9,17},{17,25},{2,10},{10,18},{18,26},{... | collective-permute-start | bytes 36872 | tf_op jit(solution)/shard_map/while/body/eval_jaxpr/ppermute | solution.py:23
  1014.5 33.8 %collective-permute-start.2 = (bf16[24,64]{1,0:T(8,128)(2,1)S(1)}, bf16[24,64]{1,0:T(8,128)(2,1)S(1)}, u32[]{:S(2)}, u32[]{:S(2)}) collective-permute-start(bf16[24,64]{1,0:T(8,128)(2,1)S(1)} %convert_element_type.84), channel_id=1, source_target_pairs={{0,8},{8,16},{16,24},{1,9},{9,17},{17,25},{2,10},{10,18},{18,26},{... | collective-permute-start | bytes 9224 | tf_op jit(solution)/shard_map/while/body/eval_jaxpr/ppermute | solution.py:23
  (28 other events, 57.5 us)
Sparse Core Ops, SparseCore 0:
  9.0 246.8 all-gather.1
where the time goes:
time: 1060 us
  waiting for transfers between devices  747 us (70%)
  matrix products  121 us (11%)
  local copies, waits for them, and re-layouts  116 us (11%)
  other arithmetic  39.8 us (4%)
  starting transfers between devices  19.3 us (2%)
  between operations  13.4 us (1%)
    ppermute x15, waiting for transfers between devices, shifted(): return lax.ppermute(block, axis, route)  499 us
    all_gather x1, waiting for transfers between devices, on_device(): full_weight = lax.all_gather(proj_weight, 'dp', axis=0, tiled=True)  247 us
    dynamic_slice x24, local copies, waits for them, and re-layouts, run_slab(): lax.scan(minibatch, start_state, (inputs[0], inputs[1], inputs[2], step_r...  56.6 us
  transfers between devices with their start and end apart: 16, of which 6 were waited for; matrix products, arithmetic and copies ran while one was open for 0% of the time, Pallas kernels for 0%

commit v1 on v0

v1 whole, which is shorter than its diff:
```python
import functools
import math

import jax
import jax.numpy as jnp
from jax import lax
from jax.experimental import pallas as pl
from jax.experimental.pallas import tpu as pltpu
from jax.sharding import PartitionSpec as P

MB = 64
PAIR = 2
coefficient = 0.044715
root_scale = math.sqrt(2.0 / math.pi)
f32 = jnp.float32
bf16 = jnp.bfloat16


def gelu_value(z):
    u = z * z
    t = jnp.tanh(z * (root_scale + (root_scale * coefficient) * u))
    h = 0.5 * z
    return h + h * t


def gelu_pair(z):
    u = z * z
    t = jnp.tanh(z * (root_scale + (root_scale * coefficient) * u))
    h = 0.5 * z
    value = h + h * t
    slope = (0.5 + 0.5 * t) + h * (1.0 - t * t) * (
        root_scale + (3.0 * root_scale * coefficient) * u
    )
    return value, slope


def dot(a, b):
    return jnp.dot(a, b, preferred_element_type=f32)


def dot_t(a, b):
    return lax.dot_general(a, b, (((1,), (1,)), ((), ())), preferred_element_type=f32)


def block_masks(width, step):
    rows = lax.broadcasted_iota(jnp.int32, (width, width), 0)
    cols = lax.broadcasted_iota(jnp.int32, (width, width), 1)
    same = (rows // step) == (cols // step)
    return same, same & (cols <= rows)


def ttt_step(read, state, rate_row, gain_row, masks, blocks):
    same, causal = masks
    w1_ref, b1_ref, w2_ref, b2_ref = state
    step = MB
    width = blocks * step
    q, k, v = read
    zero = jnp.zeros((), bf16)
    k_bd = jnp.where(same, jnp.concatenate([k] * blocks, axis=0), zero)
    q_bd = jnp.where(same, jnp.concatenate([q] * blocks, axis=0), zero)
    w1 = w1_ref[...]
    w2 = w2_ref[...]
    w1_low = w1.astype(bf16)
    w2_low = w2.astype(bf16)
    b1 = b1_ref[...]
    b2 = b2_ref[0:1, :]
    b1_rows = jnp.concatenate(
        [jnp.broadcast_to(b1[i : i + 1], (step, b1.shape[1])) for i in range(blocks)], axis=0
    )
    z1 = dot(k_bd, w1_low) + b1_rows
    x2, slope = gelu_pair(z1)
    x2_low = x2.astype(bf16)
    target = b2 - (v.astype(f32) - k.astype(f32))
    z2 = dot_t(x2_low, w2_low)
    g2 = jnp.where(same, z2 + jnp.concatenate([target] * blocks, axis=0), 0.0)
    g2_low = g2.astype(bf16)
    g1_low = (dot(g2_low, w2_low) * slope).astype(bf16)
    m1 = jnp.where(causal, (dot_t(q_bd, k_bd) + 1.0) * rate_row, 0.0).astype(bf16)
    z1q = dot(q_bd, w1_low) + b1_rows - dot(m1, g1_low)
    x2q_low = gelu_value(z1q).astype(bf16)
    m2 = jnp.where(causal, (dot_t(x2q_low, x2_low) + 1.0) * rate_row, 0.0).astype(bf16)
    z2q = dot_t(x2q_low, w2_low) - dot(m2, g2_low)
    lane = lax.broadcasted_iota(jnp.int32, (step, width), 1) // step
    out = z2q[:step]
    for i in range(1, blocks):
        out = jnp.where(lane == i, z2q[i * step : (i + 1) * step], out)
    y = q.astype(f32) + out + b2
    member = lax.broadcasted_iota(jnp.int32, (8, width), 0)
    rate_bd = jnp.where(
        member == lax.broadcasted_iota(jnp.int32, (8, width), 1) // step, rate_row, 0.0
    ).astype(bf16)
    k_scaled = (k_bd.astype(f32).T * rate_row).astype(bf16)
    g2_scaled = (g2.T * rate_row).astype(bf16)
    w1_ref[...] = w1 - dot(k_scaled, g1_low)
    b1_ref[...] = b1 - dot(rate_bd, g1_low)
    w2_ref[...] = w2 - dot(g2_scaled, x2_low)
    db2 = dot(rate_bd, g2_low)
    b2_ref[0:1, :] = b2 - jnp.sum(db2, axis=0, keepdims=True)
    square = dot((y * y).astype(bf16), same.astype(bf16)) * (1.0 / step)
    return y * lax.rsqrt(square + 1e-06) * gain_row


def round_state(state):
    for ref in state:
        ref[...] = ref[...].astype(bf16).astype(f32)


def ttt_kernel(groups, clips, proj_ref, rate_ref, w1_in, b1_in, w2_in, b2_in, gain_ref, out_ref, *scratch):
    blocks = clips * PAIR
    slabs = proj_ref.shape[0]
    batches = proj_ref.shape[2] // MB
    lanes = PAIR * MB
    states = [scratch[4 * g : 4 * g + 4] for g in range(groups)]
    for g in range(groups):
        for c in range(clips):
            states[g][0][c * lanes : (c + 1) * lanes, :] = w1_in[g]
            states[g][2][c * lanes : (c + 1) * lanes, :] = w2_in[g]
        states[g][1][...] = b1_in[g]
        states[g][3][...] = b2_in[g]

    def slab_body(s, carry):
        masks = block_masks(blocks * MB, MB)
        for b in range(batches):
            for g in range(groups):
                read = [
                    jnp.concatenate(
                        [
                            proj_ref[s, c, b * MB : (b + 1) * MB, (3 * g + part) * lanes : (3 * g + part + 1) * lanes]
                            for c in range(clips)
                        ],
                        axis=1,
                    )
                    for part in range(3)
                ]
                y = ttt_step(
                    read, states[g], rate_ref[g, s * batches + b], gain_ref[g], masks, blocks
                ).astype(bf16)
                for c in range(clips):
                    out_ref[s, c, b * MB : (b + 1) * MB, g * lanes : (g + 1) * lanes] = y[
                        :, c * lanes : (c + 1) * lanes
                    ]
        for g in range(groups):
            round_state(states[g])
        return carry

    lax.fori_loop(0, slabs, slab_body, 0)


def on_device(
    frames,
    proj_weight,
    rate_weight,
    rate_bias,
    init_weights,
    init_bias_hidden,
    init_bias_out,
    out_gain,
):
    clips, slab_len, model_width = frames.shape
    heads = rate_weight.shape[1]
    size = init_weights.shape[2]
    inner = init_weights.shape[3]
    length = lax.axis_size("seq")
    position = lax.axis_index("seq")
    mine = heads // length
    groups = -(-mine // PAIR)
    padded = groups * PAIR
    lanes = PAIR * size
    blocks = clips * PAIR
    batches = slab_len // MB
    first = position * mine

    def own(array, axis):
        part = lax.dynamic_slice_in_dim(array, first, mine, axis)
        pads = [(0, 0)] * array.ndim
        pads[axis] = (0, padded - mine)
        return jnp.pad(part, pads) if padded > mine else part

    weight = own(proj_weight.reshape(-1, 3, heads, size), 2)
    weight = weight.reshape(-1, 3, groups, lanes).transpose(0, 2, 1, 3).reshape(-1, groups * 3 * lanes)
    weight = lax.all_gather(weight, "dp", axis=0, tiled=True)
    all_frames = lax.all_gather(frames, "seq", axis=0)
    rows = all_frames.reshape(length * clips * slab_len, model_width)
    projected = jnp.dot(rows, weight, preferred_element_type=f32).astype(bf16)
    projected = projected.reshape(length, clips, slab_len, groups * 3 * lanes)
    rates = jnp.dot(rows, own(rate_weight, 1), preferred_element_type=f32)
    rates = jax.nn.sigmoid(rates + own(rate_bias, 0)) / (MB * (size + inner))
    rates = rates.reshape(length, clips, batches, MB, groups, PAIR).transpose(4, 0, 2, 1, 5, 3)
    rates = rates.reshape(groups, length * batches, 1, blocks * MB)
    w_own = own(init_weights, 1).reshape(2, groups, lanes, inner)
    b1 = own(init_bias_hidden, 0).reshape(groups, 1, PAIR, inner)
    b1 = jnp.broadcast_to(b1, (groups, clips, PAIR, inner)).reshape(groups, blocks, inner)
    b1 = jnp.pad(b1, ((0, 0), (0, 8 - blocks), (0, 0)))
    b2 = own(init_bias_out, 0).reshape(groups, 1, 1, lanes)
    b2 = jnp.broadcast_to(b2, (groups, 8, clips, lanes)).reshape(groups, 8, blocks * size)
    gain = own(out_gain.reshape(heads, size), 0).reshape(groups, 1, 1, lanes)
    gain = jnp.broadcast_to(gain, (groups, 1, clips, lanes)).reshape(groups, 1, blocks * size)

    results = pl.pallas_call(
        functools.partial(ttt_kernel, groups, clips),
        out_shape=jax.ShapeDtypeStruct((length, clips, slab_len, groups * lanes), bf16),
        in_specs=[pl.BlockSpec(memory_space=pltpu.VMEM)] * 7,
        out_specs=pl.BlockSpec(memory_space=pltpu.VMEM),
        scratch_shapes=[
            pltpu.VMEM((blocks * size, inner), f32),
            pltpu.VMEM((8, inner), f32),
            pltpu.VMEM((blocks * size, inner), f32),
            pltpu.VMEM((8, blocks * size), f32),
        ]
        * groups,
        compiler_params=pltpu.CompilerParams(vmem_limit_bytes=48 * 1024 * 1024),
        name="fast_state",
    )(projected, rates, w_own[0], b1, w_own[1], b2, gain)

    exchanged = lax.all_to_all(results, "seq", 0, 0)
    exchanged = exchanged[..., : mine * size]
    return exchanged.transpose(1, 2, 0, 3).reshape(clips, slab_len, heads * size)


def solution(mesh):
    return jax.shard_map(
        on_device,
        mesh=mesh,
        in_specs=(P("dp", "seq", None), P("dp", None), P(), P(), P(), P(), P(), P()),
        out_specs=P("dp", "seq", None),
        check_vma=False,
    )
```

time: 1060 us -> 215 us (0.20)
  the two profiles are of different devices: /device:TPU:6 before, /device:TPU:0 now
where the time goes in v1:
time: 215 us; the launch traced here: 214 us
  waiting for transfers between devices  132 us (61%)
  Pallas kernels  23.5 us (11%)
  matrix products  17 us (8%)
  blocking collectives  15.2 us (7%)
  between operations  13.5 us (6%)
  local copies, waits for them, and re-layouts  12.8 us (6%)
    all_gather x1, waiting for transfers between devices, on_device(): weight = lax.all_gather(weight, 'dp', axis=0, tiled=True)  68 us
    all_gather x1, waiting for transfers between devices, on_device(): all_frames = lax.all_gather(frames, 'seq', axis=0)  63.7 us
    pallas_call x1, Pallas kernels, on_device(): pl.pallas_call(functools.partial(ttt_kernel, groups, clips), out_shape=ja...  23.5 us
    all_to_all x1, blocking collectives, on_device(): exchanged = lax.all_to_all(results, 'seq', 0, 0)  15.2 us
    dot_general x1, matrix products, on_device(): projected = jnp.dot(rows, weight, preferred_element_type=f32).astype(bf16)  12.5 us
    unnamed x9, local copies, waits for them, and re-layouts  5.76 us
    dot_general x1, matrix products, on_device(): rates = jnp.dot(rows, own(rate_weight, 1), preferred_element_type=f32)  4.53 us
  transfers between devices with their start and end apart: 2, of which 2 were waited for; matrix products, arithmetic and copies ran while one was open for 7% of the time, Pallas kernels for 0%

profile of v1, /device:TPU:0, one launch (start us, length us, event | category | flops | bytes accessed | tf_op | source)
XLA Modules:
  0.0 214.5 jit_solution(4206196702932382474)
XLA Ops:
  6.5 0.0 copy-start
  6.5 0.0 copy-start.2
  6.5 0.0 copy-start.1
  6.5 0.0 all-gather.6.cloned.1.call-start
  6.5 0.7 all-gather.6.cloned.1.call-update
  7.3 0.0 all-gather.4.cloned.1.call-start
  7.3 5.7 %copy.15 = bf16[384,4608]{0,1:T(8,128)(2,1)} copy(bf16[384,4608]{1,0:T(8,128)(2,1)} %param.9) | data formatting | bytes 7077888 | tf_op args[1]
  13.1 1.3 constant_dynamic-slice_fusion.5
  14.3 1.0 copy.16
  15.3 0.0 all-gather.4.cloned.1.call-update
  15.4 0.0 copy-done.2
  15.4 0.1 dynamic_slice.23
  15.5 0.7 constant_dynamic-slice_fusion.3
  16.2 0.0 copy-done.1
  16.2 0.1 reshape.58
  16.3 0.7 constant_dynamic-slice_fusion.1
  17.0 0.1 broadcast_in_dim.30
  17.1 0.1 broadcast_in_dim.34
  17.2 1.2 constant_dynamic-slice_fusion.4
  18.4 63.7 %all-gather.6.cloned.1.call-done = bf16[8,128,3072]{2,1,0:T(8,128)(2,1)} async-done(((bf16[2,128,3072]{2,1,0:T(8,128)(2,1)}), bf16[8,128,3072]{2,1,0:T(8,128)(2,1)}) %all-gather.6.cloned.1.call-update) | async-done | bytes 6291472 | tf_op jit(solution)/shard_map/all_gather | solution.py:182
  82.1 0.0 copy-done
  82.1 4.5 %fusion.5 = f32[1024,6]{0,1:T(8,128)S(1)} fusion(bf16[1024,3072]{1,0:T(8,128)(2,1)} %bitcast.33, bf16[3072,24]{0,1:T(8,128)(2,1)S(1)} %copy-done, s32[]{:T(128)S(6)} %select_n.2, f32[6]{0:T(128)S(1)} %dynamic_slice.23), kind=kOutput, calls=%fused_computation.7 | convolution fusion | flops 37779456 | bytes 6365700 | tf_op jit(solution)/shard_map/dot_general | solution.py:186
  86.6 0.1 reshape.55
  86.8 0.1 reshape.56.rate_ref
  86.9 68.0 %all-gather.4.cloned.1.call-done = bf16[3072,1152]{0,1:T(8,128)(2,1)} async-done(((bf16[384,1152]{0,1:T(8,128)(2,1)}), bf16[3072,1152]{0,1:T(8,128)(2,1)}) %all-gather.4.cloned.1.call-update) | async-done | bytes 7077904 | tf_op jit(solution)/shard_map/all_gather | solution.py:181
  154.9 12.5 %convolution_convert_fusion = bf16[1152,1024]{0,1:T(8,128)(2,1)S(1)} fusion(bf16[3072,1152]{0,1:T(8,128)(2,1)} %all-gather.4.cloned.1.call-done, bf16[1024,3072]{1,0:T(8,128)(2,1)} %bitcast.34), kind=kOutput, calls=%fused_computation | convolution fusion | flops 7248936960 | bytes 15728640 | tf_op jit(solution)/shard_map/dot_general | solution.py:184
  167.4 23.5 %fast_state.1 = bf16[4,2,128,384]{3,2,1,0:T(8,128)(2,1)S(1)} custom-call(bf16[4,2,128,1152]{3,2,1,0:T(8,128)(2,1)S(1)} %bitcast.29, f32[3,8,1,256]{3,2,1,0:T(1,128)S(1)} %reshape.56.rate_ref, f32[3,128,256]{2,1,0:T(8,128)S(1)} %bitcast.31, f32[3,8,256]{2,1,0:T(8,128)S(1)} %pad.4.b1_in, f32[3,128,256]{2,1,0:T(8,128)S(1)} %bitcast.30, ...), custom_call_target="tpu_custom_call" | custom-call | tf_op jit(solution)/shard_map/fast_state/pallas_call | solution.py:199
  190.9 15.2 %all_to_all.5 = bf16[4,2,128,384]{3,2,1,0:T(8,128)(2,1)S(1)} all-to-all(bf16[4,2,128,384]{3,2,1,0:T(8,128)(2,1)S(1)} %fast_state.1), channel_id=1, replica_groups=mesh['seq'=4,'dp'=8] {'seq'}, dimensions={0} | all-to-all | bytes 1572864 | tf_op jit(solution)/shard_map/all_to_all | solution.py:215
  206.1 0.4 copy.18
  206.5 1.2 copy.19
  (9 shorter events, 0.1 us)
Async XLA Ops:
  6.5 75.6 %copy-start = (bf16[3072,24]{0,1:T(8,128)(2,1)S(1)}, bf16[3072,24]{0,1:T(8,128)(2,1)}, u32[]{:S(2)}) copy-start(bf16[3072,24]{0,1:T(8,128)(2,1)} %param.10) | copy-start | bytes 442372
  6.5 8.8 %copy-start.2 = (f32[24]{0:T(128)S(1)}, f32[24]{0:T(128)}, u32[]{:S(2)}) copy-start(f32[24]{0:T(128)} %param.11) | copy-start | bytes 292
  6.5 9.7 %copy-start.1 = (f32[1536]{0:T(1024)S(1)}, f32[1536]{0:T(1024)}, u32[]{:S(2)}) copy-start(f32[1536]{0:T(1024)} %param.15) | copy-start | bytes 18436
  6.5 75.6 %all-gather.6.cloned.1.call-start = ((), (), s32[]{:S(2)}) async-start(), calls=%async_computation.2 | async-start | bytes 7864320 | tf_op jit(solution)/shard_map/all_gather | solution.py:182
  7.3 147.6 %all-gather.4.cloned.1.call-start = ((), (), s32[]{:S(2)}) async-start(), calls=%async_computation.1 | async-start | bytes 7962624 | tf_op jit(solution)/shard_map/all_gather | solution.py:181
Sparse Core Ops, SparseCore 0:
  9.2 72.8 all-gather.5
  83.7 71.1 all-gather.3

commit v2 on v1

--- a/solution.py
+++ b/solution.py
@@ -125,7 +125,7 @@
                 read = [
                     jnp.concatenate(
                         [
-                            proj_ref[s, c, b * MB : (b + 1) * MB, (3 * g + part) * lanes : (3 * g + part + 1) * lanes]
+                            proj_ref[s, c, b * MB : (b + 1) * MB, (part * groups + g) * lanes : (part * groups + g + 1) * lanes]
                             for c in range(clips)
                         ],
                         axis=1,
@@ -144,6 +144,216 @@
         return carry
 
     lax.fori_loop(0, slabs, slab_body, 0)
+
+
+def gather_kernel(
+    n_seq, n_dp, f_ref, w_ref, f_all, w_all, f_send, f_recv, w_send, w_recv, own_sem
+):
+    seq, dp = lax.axis_index("seq"), lax.axis_index("dp")
+    a, b = seq // 2, lax.rem(seq, 2)
+    z, c = dp // 2, lax.rem(dp, 2)
+    n_a, n_c = n_seq // 2, n_dp // 2
+    peers = [lax.rem(a + i, n_a) * 2 + b for i in range(1, n_a)]
+    pair = a * 2 + 1 - b
+    sibling = z * 2 + 1 - c
+    has_right, has_left = z + 1 < n_c, z > 0
+
+    own_f = pltpu.make_async_copy(f_ref, f_all.at[seq], own_sem.at[0])
+    own_w = pltpu.make_async_copy(w_ref, w_all.at[dp], own_sem.at[1])
+    own_f.start()
+    own_w.start()
+
+    barrier = pltpu.get_barrier_semaphore()
+    for other in peers + [pair]:
+        pl.semaphore_signal(
+            barrier, inc=1, device_id={"seq": other}, device_id_type=pl.DeviceIdType.MESH
+        )
+    pl.semaphore_signal(
+        barrier, inc=1, device_id={"dp": sibling}, device_id_type=pl.DeviceIdType.MESH
+    )
+
+    @pl.when(has_right)
+    def _():
+        pl.semaphore_signal(
+            barrier, inc=1, device_id={"dp": dp + 2}, device_id_type=pl.DeviceIdType.MESH
+        )
+
+    @pl.when(has_left)
+    def _():
+        pl.semaphore_signal(
+            barrier, inc=1, device_id={"dp": dp - 2}, device_id_type=pl.DeviceIdType.MESH
+        )
+
+    neighbours = jnp.where(has_right, 1, 0) + jnp.where(has_left, 1, 0)
+    pl.semaphore_wait(barrier, neighbours + (len(peers) + 2))
+
+    pending = []
+
+    def send_f(source, owner, half, to):
+        copy = pltpu.make_async_remote_copy(
+            source,
+            f_all.at[owner, half],
+            f_send.at[len(pending)],
+            f_recv.at[owner, half],
+            device_id={"seq": to},
+            device_id_type=pl.DeviceIdType.MESH,
+        )
+        copy.start()
+        pending.append(copy)
+
+    def got_f(owner, half):
+        pltpu.make_async_remote_copy(
+            f_all.at[owner, half],
+            f_all.at[owner, half],
+            f_send.at[0],
+            f_recv.at[owner, half],
+            device_id={"seq": pair},
+            device_id_type=pl.DeviceIdType.MESH,
+        ).wait_recv()
+
+    def copy_w(source, owner, piece, way, distance):
+        to = (dp + 2, dp - 2, sibling)[way]
+        return pltpu.make_async_remote_copy(
+            source,
+            w_all.at[owner, piece],
+            w_send.at[(way * n_c + distance) * 2 + piece],
+            w_recv.at[owner, piece],
+            device_id={"dp": to},
+            device_id_type=pl.DeviceIdType.MESH,
+        )
+
+    def got_w(owner, piece):
+        copy_w(w_all.at[owner, piece], owner, piece, 2, 0).wait_recv()
+
+    for piece in range(2):
+
+        @pl.when(has_right)
+        def _():
+            copy_w(w_ref.at[piece], dp, piece, 0, 0).start()
+
+        @pl.when(has_left)
+        def _():
+            copy_w(w_ref.at[piece], dp, piece, 1, 0).start()
+
+    for half in (0, 1):
+        for other in peers:
+            send_f(f_ref.at[half], seq, half, other)
+        send_f(f_ref.at[1 - half], seq, 1 - half, pair)
+    for piece in range(2):
+        copy_w(w_ref.at[piece], dp, piece, 2, 0).start()
+
+    for distance in range(1, n_c):
+        for piece in range(2):
+            for way, sign, here, onward in (
+                (0, -1, z >= distance, has_right),
+                (1, 1, z + distance < n_c, has_left),
+            ):
+                owner = dp + sign * 2 * distance
+
+                @pl.when(here)
+                def _():
+                    got_w(owner, piece)
+
+                    @pl.when(onward)
+                    def _():
+                        copy_w(w_all.at[owner, piece], owner, piece, way, distance).start()
+
+                    share(w_all, w_send, w_recv, owner, piece, way, distance, n_c, sibling).start()
+
+            if distance == 1 and piece == 0:
+                relay_f(peers, pair, got_f, send_f, f_all)
+    if n_c == 1:
+        relay_f(peers, pair, got_f, send_f, f_all)
+
+    for other in peers:
+        got_f(other, 1)
+        far = other + 1 - 2 * b
+        got_f(far, 0)
+        got_f(far, 1)
+    got_f(pair, 0)
+    for chip in range(n_c):
+        for piece in range(2):
+            got_w(chip * 2 + 1 - c, piece)
+
+    for copy in pending:
+        copy.wait_send()
+    for piece in range(2):
+
+        @pl.when(has_right)
+        def _():
+            copy_w(w_ref.at[piece], dp, piece, 0, 0).wait_send()
+
+        @pl.when(has_left)
+        def _():
+            copy_w(w_ref.at[piece], dp, piece, 1, 0).wait_send()
+
+        copy_w(w_ref.at[piece], dp, piece, 2, 0).wait_send()
+        for distance in range(1, n_c):
+            for way, sign, here, onward in (
+                (0, -1, z >= distance, has_right),
+                (1, 1, z + distance < n_c, has_left),
+            ):
+                owner = dp + sign * 2 * distance
+
+                @pl.when(here)
+                def _():
+                    @pl.when(onward)
+                    def _():
+                        copy_w(w_all.at[owner, piece], owner, piece, way, distance).wait_send()
+
+                    share(
+                        w_all, w_send, w_recv, owner, piece, way, distance, n_c, sibling
+                    ).wait_send()
+
+    own_f.wait()
+    own_w.wait()
+
+
+def relay_f(peers, pair, got_f, send_f, f_all):
+    for other in peers:
+        got_f(other, 0)
+        send_f(f_all.at[other, 0], other, 0, pair)
+    got_f(pair, 1)
+    for other in peers:
+        send_f(f_all.at[pair, 1], pair, 1, other)
+
+
+def share(w_all, w_send, w_recv, owner, piece, way, distance, n_c, sibling):
+    return pltpu.make_async_remote_copy(
+        w_all.at[owner, piece],
+        w_all.at[owner, piece],
+        w_send.at[((2 + way) * n_c + distance) * 2 + piece],
+        w_recv.at[owner, piece],
+        device_id={"dp": sibling},
+        device_id_type=pl.DeviceIdType.MESH,
+    )
+
+
+def gather_both(frames, weight, n_seq, n_dp):
+    clips, slab_len, width = frames.shape
+    depth, columns = weight.shape
+    n_a, n_c = n_seq // 2, n_dp // 2
+    halves = frames.reshape(2, clips * slab_len // 2, width)
+    pieces = weight.reshape(2, depth // 2, columns)
+    f_all, w_all = pl.pallas_call(
+        functools.partial(gather_kernel, n_seq, n_dp),
+        out_shape=(
+            jax.ShapeDtypeStruct((n_seq,) + halves.shape, bf16),
+            jax.ShapeDtypeStruct((n_dp,) + pieces.shape, bf16),
+        ),
+        in_specs=[pl.BlockSpec(memory_space=pl.ANY)] * 2,
+        out_specs=(pl.BlockSpec(memory_space=pl.ANY),) * 2,
+        scratch_shapes=[
+            pltpu.SemaphoreType.DMA((2 * n_a + 2 * (n_a - 1),)),
+            pltpu.SemaphoreType.DMA((n_seq, 2)),
+            pltpu.SemaphoreType.DMA((4 * n_c * 2,)),
+            pltpu.SemaphoreType.DMA((n_dp, 2)),
+            pltpu.SemaphoreType.DMA((2,)),
+        ],
+        compiler_params=pltpu.CompilerParams(collective_id=0, has_side_effects=True),
+        name="gather_both",
+    )(halves, pieces)
+    return f_all.reshape(n_seq * clips * slab_len, width), w_all.reshape(n_dp * depth, columns)
 
 
 def on_device(
@@ -176,11 +386,15 @@
         pads[axis] = (0, padded - mine)
         return jnp.pad(part, pads) if padded > mine else part
 
-    weight = own(proj_weight.reshape(-1, 3, heads, size), 2)
-    weight = weight.reshape(-1, 3, groups, lanes).transpose(0, 2, 1, 3).reshape(-1, groups * 3 * lanes)
-    weight = lax.all_gather(weight, "dp", axis=0, tiled=True)
-    all_frames = lax.all_gather(frames, "seq", axis=0)
-    rows = all_frames.reshape(length * clips * slab_len, model_width)
+    span = proj_weight.shape[1] // 3
+    parts = [
+        lax.dynamic_slice_in_dim(proj_weight, part * span + first * size, mine * size, 1)
+        for part in range(3)
+    ]
+    if padded > mine:
+        parts = [jnp.pad(part, ((0, 0), (0, (padded - mine) * size))) for part in parts]
+    weight = jnp.concatenate(parts, axis=1)
+    rows, weight = gather_both(frames, weight, length, lax.axis_size("dp"))
     projected = jnp.dot(rows, weight, preferred_element_type=f32).astype(bf16)
     projected = projected.reshape(length, clips, slab_len, groups * 3 * lanes)
     rates = jnp.dot(rows, own(rate_weight, 1), preferred_element_type=f32)

time: 215 us -> 140 us (0.65)
  waiting for transfers between devices: 132 us -> 0 us
  Pallas kernels: 23.5 us -> 99.6 us
  between operations: 13.5 us -> 0.13 us
  local copies, waits for them, and re-layouts: 12.8 us -> 6.02 us
    all_gather x2 -> x0, waiting for transfers between devices: 132 us -> none  [the longest x1 68 us: on_device(): weight = lax.all_gather(weight, 'dp', axis=0, tiled=True)]
    pallas_call x0 -> x1, Pallas kernels: none -> 76.1 us  [gather_both(): pl.pallas_call(functools.partial(gather_kernel, n_seq, n_dp), out_shape=(...]
    unnamed x9 -> x8, local copies, waits for them, and re-layouts: 5.76 us -> 0.03 us
  transfers between devices with their start and end apart: 2 -> 0, of which waited for: 2 -> 0; matrix products, arithmetic and copies ran while one was open for 7% -> 0% of each run, Pallas kernels for 0% -> 0%
where the time goes in v2:
time: 140 us
  Pallas kernels  99.6 us (71%)
  matrix products  17 us (12%)
  blocking collectives  16.2 us (12%)
  local copies, waits for them, and re-layouts  6.02 us (4%)
    pallas_call x1, Pallas kernels, gather_both(): pl.pallas_call(functools.partial(gather_kernel, n_seq, n_dp), out_shape=(...  76.1 us
    pallas_call x1, Pallas kernels, on_device(): pl.pallas_call(functools.partial(ttt_kernel, groups, clips), out_shape=ja...  23.5 us
    all_to_all x1, blocking collectives, on_device(): exchanged = lax.all_to_all(results, 'seq', 0, 0)  16.2 us
    dot_general x1, matrix products, on_device(): projected = jnp.dot(rows, weight, preferred_element_type=f32).astype(bf16)  12.5 us
    dot_general x1, matrix products, on_device(): rates = jnp.dot(rows, own(rate_weight, 1), preferred_element_type=f32)  4.53 us

profile of v2, /device:TPU:0, one launch (start us, length us, event | category | flops | bytes accessed | tf_op | source)
XLA Modules:
  0.0 140.0 jit_solution(10338871198188259548)
XLA Ops:
  0.0 0.0 copy-start
  0.0 1.3 constant_dynamic-slice_fusion.7
  1.3 1.0 pad_maximum_fusion
  2.3 76.1 %gather_both.1 = (bf16[4,2,128,3072]{3,2,1,0:T(8,128)(2,1)}, bf16[8,2,192,1152]{3,2,1,0:T(8,128)(2,1)}) custom-call(bf16[2,128,3072]{2,1,0:T(8,128)(2,1)} %f_ref.1, bf16[2,192,1152]{2,1,0:T(8,128)(2,1)} %bitcast.28), custom_call_target="tpu_custom_call" | custom-call | tf_op jit(solution)/shard_map/gather_both/pallas_call | solution.py:338
  78.4 0.0 copy-start.2
  78.4 12.5 %convolution_convert_fusion = bf16[1024,1152]{1,0:T(8,128)(2,1)S(1)} fusion(bf16[1024,3072]{1,0:T(8,128)(2,1)} %bitcast.26, bf16[3072,1152]{1,0:T(8,128)(2,1)} %bitcast.33), kind=kOutput, calls=%fused_computation | convolution fusion | flops 7248936960 | bytes 15728640 | tf_op jit(solution)/shard_map/dot_general | solution.py:398
  90.9 0.0 copy-start.1
  90.9 0.0 copy-done.2
  90.9 0.1 dynamic_slice.31
  91.0 0.0 copy-done
  91.0 4.5 %fusion.4 = f32[1024,6]{0,1:T(8,128)S(1)} fusion(bf16[1024,3072]{1,0:T(8,128)(2,1)} %bitcast.27, bf16[3072,24]{0,1:T(8,128)(2,1)S(1)} %copy-done, s32[]{:T(128)S(6)} %select_n.20, f32[6]{0:T(128)S(1)} %dynamic_slice.31), kind=kOutput, calls=%fused_computation.6 | convolution fusion | flops 37779456 | bytes 6365700 | tf_op jit(solution)/shard_map/dot_general | solution.py:400
  95.5 0.1 reshape.51
  95.6 0.1 reshape.52.rate_ref
  95.8 0.0 copy-done.1
  95.8 0.1 reshape.54
  95.8 0.7 constant_dynamic-slice_fusion.1
  96.5 0.1 broadcast_in_dim.30
  96.6 0.1 broadcast_in_dim.34
  96.7 0.7 constant_dynamic-slice_fusion.3
  97.5 1.2 constant_dynamic-slice_fusion.4
  98.7 23.5 %fast_state.1 = bf16[4,2,128,384]{3,2,1,0:T(8,128)(2,1)S(1)} custom-call(bf16[4,2,128,1152]{3,2,1,0:T(8,128)(2,1)S(1)} %bitcast.22, f32[3,8,1,256]{3,2,1,0:T(1,128)S(1)} %reshape.52.rate_ref, f32[3,128,256]{2,1,0:T(8,128)S(1)} %bitcast.24, f32[3,8,256]{2,1,0:T(8,128)S(1)} %pad.4.b1_in, f32[3,128,256]{2,1,0:T(8,128)S(1)} %bitcast.23, ...), custom_call_target="tpu_custom_call" | custom-call | tf_op jit(solution)/shard_map/fast_state/pallas_call | solution.py:413
  122.2 16.2 %all_to_all.5 = bf16[4,2,128,384]{3,2,1,0:T(8,128)(2,1)S(1)} all-to-all(bf16[4,2,128,384]{3,2,1,0:T(8,128)(2,1)S(1)} %fast_state.1), channel_id=1, replica_groups=mesh['seq'=4,'dp'=8] {'seq'}, dimensions={0} | all-to-all | bytes 1572864 | tf_op jit(solution)/shard_map/all_to_all | solution.py:429
  138.4 0.4 copy.11
  138.8 1.2 copy.12
  (9 shorter events, 0.1 us)
Async XLA Ops:
  0.0 91.0 %copy-start = (bf16[3072,24]{0,1:T(8,128)(2,1)S(1)}, bf16[3072,24]{0,1:T(8,128)(2,1)}, u32[]{:S(2)}) copy-start(bf16[3072,24]{0,1:T(8,128)(2,1)} %param.10) | copy-start | bytes 442372
  78.4 12.5 %copy-start.2 = (f32[24]{0:T(128)S(1)}, f32[24]{0:T(128)}, u32[]{:S(2)}) copy-start(f32[24]{0:T(128)} %param.11) | copy-start | bytes 292
  90.9 4.9 %copy-start.1 = (f32[1536]{0:T(1024)S(1)}, f32[1536]{0:T(1024)}, u32[]{:S(2)}) copy-start(f32[1536]{0:T(1024)} %param.15) | copy-start | bytes 18436

commit v3 on v2

--- a/solution.py
+++ b/solution.py
@@ -260,7 +260,7 @@
 
                     share(w_all, w_send, w_recv, owner, piece, way, distance, n_c, sibling).start()
 
-            if distance == 1 and piece == 0:
+            if distance == 1 and piece == 1:
                 relay_f(peers, pair, got_f, send_f, f_all)
     if n_c == 1:
         relay_f(peers, pair, got_f, send_f, f_all)
@@ -356,6 +356,59 @@
     return f_all.reshape(n_seq * clips * slab_len, width), w_all.reshape(n_dp * depth, columns)
 
 
+def exchange_kernel(n_seq, source, result, send, recv, own_sem):
+    me = lax.axis_index("seq")
+    own = pltpu.make_async_copy(source.at[me], result.at[me], own_sem.at[0])
+    own.start()
+    barrier = pltpu.get_barrier_semaphore()
+    others = [lax.rem(me + i, n_seq) for i in range(1, n_seq)]
+    for other in others:
+        pl.semaphore_signal(
+            barrier, inc=1, device_id={"seq": other}, device_id_type=pl.DeviceIdType.MESH
+        )
+    pl.semaphore_wait(barrier, n_seq - 1)
+    copies = []
+    for i, other in enumerate(others):
+        copy = pltpu.make_async_remote_copy(
+            source.at[other],
+            result.at[me],
+            send.at[i],
+            recv.at[me],
+            device_id={"seq": other},
+            device_id_type=pl.DeviceIdType.MESH,
+        )
+        copy.start()
+        copies.append(copy)
+    for other in others:
+        pltpu.make_async_remote_copy(
+            source.at[other],
+            result.at[other],
+            send.at[0],
+            recv.at[other],
+            device_id={"seq": other},
+            device_id_type=pl.DeviceIdType.MESH,
+        ).wait_recv()
+    for copy in copies:
+        copy.wait_send()
+    own.wait()
+
+
+def exchange(blocks, n_seq):
+    return pl.pallas_call(
+        functools.partial(exchange_kernel, n_seq),
+        out_shape=jax.ShapeDtypeStruct(blocks.shape, blocks.dtype),
+        in_specs=[pl.BlockSpec(memory_space=pl.ANY)],
+        out_specs=pl.BlockSpec(memory_space=pl.ANY),
+        scratch_shapes=[
+            pltpu.SemaphoreType.DMA((n_seq - 1,)),
+            pltpu.SemaphoreType.DMA((n_seq,)),
+            pltpu.SemaphoreType.DMA((1,)),
+        ],
+        compiler_params=pltpu.CompilerParams(collective_id=1, has_side_effects=True),
+        name="exchange",
+    )(blocks)
+
+
 def on_device(
     frames,
     proj_weight,
@@ -426,7 +479,7 @@
         name="fast_state",
     )(projected, rates, w_own[0], b1, w_own[1], b2, gain)
 
-    exchanged = lax.all_to_all(results, "seq", 0, 0)
+    exchanged = exchange(results, length)
     exchanged = exchanged[..., : mine * size]
     return exchanged.transpose(1, 2, 0, 3).reshape(clips, slab_len, heads * size)
 

time: 140 us -> 140 us (level)
  blocking collectives: 16.2 us -> 0 us
  Pallas kernels: 99.6 us -> 113 us
  local copies, waits for them, and re-layouts: 6.02 us -> 8.05 us
    all_to_all x1 -> x0, blocking collectives: 16.2 us -> none  [on_device(): exchanged = lax.all_to_all(results, 'seq', 0, 0)]
    pallas_call x0 -> x1, Pallas kernels: none -> 13.7 us  [exchange(): pl.pallas_call(functools.partial(exchange_kernel, n_seq), out_shape=jax.S...]
where the time goes in v3:
time: 140 us; the launch traced here: 139 us
  Pallas kernels  113 us (81%)
  matrix products  17 us (12%)
  local copies, waits for them, and re-layouts  8.05 us (6%)
    pallas_call x1, Pallas kernels, gather_both(): pl.pallas_call(functools.partial(gather_kernel, n_seq, n_dp), out_shape=(...  76.1 us
    pallas_call x1, Pallas kernels, on_device(): pl.pallas_call(functools.partial(ttt_kernel, groups, clips), out_shape=ja...  23.5 us
    pallas_call x1, Pallas kernels, exchange(): pl.pallas_call(functools.partial(exchange_kernel, n_seq), out_shape=jax.S...  13.7 us
    dot_general x1, matrix products, on_device(): projected = jnp.dot(rows, weight, preferred_element_type=f32).astype(bf16)  12.4 us
    dot_general x1, matrix products, on_device(): rates = jnp.dot(rows, own(rate_weight, 1), preferred_element_type=f32)  4.53 us

profile of v3, /device:TPU:0, one launch (start us, length us, event | category | flops | bytes accessed | tf_op | source)
XLA Modules:
  0.0 139.5 jit_solution(14993641802800131264)
XLA Ops:
  0.0 0.0 copy-start
  0.0 1.3 constant_dynamic-slice_fusion.7
  1.3 1.0 pad_maximum_fusion
  2.3 76.1 %gather_both.1 = (bf16[4,2,128,3072]{3,2,1,0:T(8,128)(2,1)}, bf16[8,2,192,1152]{3,2,1,0:T(8,128)(2,1)}) custom-call(bf16[2,128,3072]{2,1,0:T(8,128)(2,1)} %f_ref.1, bf16[2,192,1152]{2,1,0:T(8,128)(2,1)} %bitcast.28), custom_call_target="tpu_custom_call" | custom-call | tf_op jit(solution)/shard_map/gather_both/pallas_call | solution.py:338
  78.4 0.0 copy-start.3
  78.4 12.4 %convolution_convert_fusion = bf16[1024,1152]{1,0:T(8,128)(2,1)S(1)} fusion(bf16[1024,3072]{1,0:T(8,128)(2,1)} %bitcast.26, bf16[3072,1152]{1,0:T(8,128)(2,1)} %bitcast.33), kind=kOutput, calls=%fused_computation | convolution fusion | flops 7248936960 | bytes 15728640 | tf_op jit(solution)/shard_map/dot_general | solution.py:451
  90.9 0.0 copy-start.2
  90.9 0.0 copy-done.3
  90.9 0.1 dynamic_slice.31
  91.0 0.0 copy-done
  91.0 4.5 %fusion.4 = f32[1024,6]{0,1:T(8,128)S(1)} fusion(bf16[1024,3072]{1,0:T(8,128)(2,1)} %bitcast.27, bf16[3072,24]{0,1:T(8,128)(2,1)S(1)} %copy-done, s32[]{:T(128)S(6)} %select_n.20, f32[6]{0:T(128)S(1)} %dynamic_slice.31), kind=kOutput, calls=%fused_computation.6 | convolution fusion | flops 37779456 | bytes 6365700 | tf_op jit(solution)/shard_map/dot_general | solution.py:453
  95.5 0.1 reshape.51
  95.7 0.1 reshape.52.rate_ref
  95.8 1.2 constant_dynamic-slice_fusion.4
  97.0 0.0 copy-done.2
  97.0 0.1 reshape.54
  97.0 0.7 constant_dynamic-slice_fusion.1
  97.7 0.1 broadcast_in_dim.30
  97.8 0.1 broadcast_in_dim.34
  97.9 0.7 constant_dynamic-slice_fusion.3
  98.7 23.5 %fast_state.1.source = bf16[4,2,128,384]{3,2,1,0:T(8,128)(2,1)S(1)} custom-call(bf16[4,2,128,1152]{3,2,1,0:T(8,128)(2,1)S(1)} %bitcast.22, f32[3,8,1,256]{3,2,1,0:T(1,128)S(1)} %reshape.52.rate_ref, f32[3,128,256]{2,1,0:T(8,128)S(1)} %bitcast.24, f32[3,8,256]{2,1,0:T(8,128)S(1)} %pad.4.b1_in, f32[3,128,256]{2,1,0:T(8,128)S(1)} %bitcast.23, ...), custom_call_target="tpu_custom_call" | custom-call | tf_op jit(solution)/shard_map/fast_state/pallas_call | solution.py:466
  122.2 0.0 copy-start.1
  122.2 0.9 copy-done.1
  123.1 13.7 %exchange.1 = bf16[4,2,128,384]{3,2,1,0:T(8,128)(2,1)} custom-call(bf16[4,2,128,384]{3,2,1,0:T(8,128)(2,1)} %copy-done.1), custom_call_target="tpu_custom_call" | custom-call | tf_op jit(solution)/shard_map/exchange/pallas_call | solution.py:397
  136.8 1.5 %copy.11 = bf16[2,128,4,384]{1,3,2,0:T(8,128)(2,1)S(1)} copy(bf16[2,128,4,384]{3,1,0,2:T(8,128)(2,1)} %bitcast.29) | data formatting | bytes 1572864 | tf_op jit(solution)/shard_map/transpose | solution.py:484
  138.3 1.2 copy.12
  (9 shorter events, 0.1 us)
Async XLA Ops:
  0.0 91.0 %copy-start = (bf16[3072,24]{0,1:T(8,128)(2,1)S(1)}, bf16[3072,24]{0,1:T(8,128)(2,1)}, u32[]{:S(2)}) copy-start(bf16[3072,24]{0,1:T(8,128)(2,1)} %param.10) | copy-start | bytes 442372
  78.4 12.5 %copy-start.3 = (f32[24]{0:T(128)S(1)}, f32[24]{0:T(128)}, u32[]{:S(2)}) copy-start(f32[24]{0:T(128)} %param.11) | copy-start | bytes 292
  90.9 6.1 %copy-start.2 = (f32[1536]{0:T(1024)S(1)}, f32[1536]{0:T(1024)}, u32[]{:S(2)}) copy-start(f32[1536]{0:T(1024)} %param.15) | copy-start | bytes 18436
  122.2 0.9 copy-start.1

commit v4 on v3

--- a/solution.py
+++ b/solution.py
@@ -147,8 +147,13 @@
 
 
 def gather_kernel(
-    n_seq, n_dp, f_ref, w_ref, f_all, w_all, f_send, f_recv, w_send, w_recv, own_sem
+    n_seq, n_dp, f_ref, w_ref, r_ref, proj_out, logit_out,
+    f_all, w_all, acc, f_send, f_recv, w_send, w_recv, own_sem
 ):
+    rows = 2 * f_ref.shape[1]
+    width = f_ref.shape[2]
+    columns = w_ref.shape[2]
+    chip_depth = 2 * 2 * w_ref.shape[1]
     seq, dp = lax.axis_index("seq"), lax.axis_index("dp")
     a, b = seq // 2, lax.rem(seq, 2)
     z, c = dp // 2, lax.rem(dp, 2)
@@ -162,6 +167,12 @@
     own_w = pltpu.make_async_copy(w_ref, w_all.at[dp], own_sem.at[1])
     own_f.start()
     own_w.start()
+
+    def zero_body(s, carry):
+        acc[s] = jnp.zeros(acc.shape[1:], f32)
+        return carry
+
+    lax.fori_loop(0, n_seq, zero_body, 0)
 
     barrier = pltpu.get_barrier_semaphore()
     for other in peers + [pair]:
@@ -242,7 +253,7 @@
     for piece in range(2):
         copy_w(w_ref.at[piece], dp, piece, 2, 0).start()
 
-    for distance in range(1, n_c):
+    def pass_on(distance):
         for piece in range(2):
             for way, sign, here, onward in (
                 (0, -1, z >= distance, has_right),
@@ -254,15 +265,32 @@
                 def _():
                     got_w(owner, piece)
 
-                    @pl.when(onward)
-                    def _():
-                        copy_w(w_all.at[owner, piece], owner, piece, way, distance).start()
+                    if distance < n_c - 1:
+
+                        @pl.when(onward)
+                        def _():
+                            copy_w(w_all.at[owner, piece], owner, piece, way, distance).start()
 
                     share(w_all, w_send, w_recv, owner, piece, way, distance, n_c, sibling).start()
 
-            if distance == 1 and piece == 1:
-                relay_f(peers, pair, got_f, send_f, f_all)
-    if n_c == 1:
+    def sibling_rows(chip):
+        for piece in range(2):
+            got_w(chip * 2 + 1 - c, piece)
+
+    def add_product(chip):
+        def body(s, carry):
+            left = f_all[s].reshape(rows, width)[:, chip * chip_depth : (chip + 1) * chip_depth]
+            right = w_all[2 * chip : 2 * chip + 2].reshape(chip_depth, columns)
+            acc[s] = acc[s] + dot(left, right)
+            return carry
+
+        lax.fori_loop(0, n_seq, body, 0)
+
+    for distance in range(1, n_c - 1):
+        pass_on(distance)
+        if distance == 1:
+            relay_f(peers, pair, got_f, send_f, f_all)
+    if n_c <= 2:
         relay_f(peers, pair, got_f, send_f, f_all)
 
     for other in peers:
@@ -271,9 +299,53 @@
         got_f(far, 0)
         got_f(far, 1)
     got_f(pair, 0)
-    for chip in range(n_c):
-        for piece in range(2):
-            got_w(chip * 2 + 1 - c, piece)
+    own_f.wait()
+    own_w.wait()
+
+    def rate_body(s, carry):
+        logit_out[s] = dot(f_all[s].reshape(rows, width), r_ref[...])
+        return carry
+
+    lax.fori_loop(0, n_seq, rate_body, 0)
+    aligned = chip_depth % 128 == 0
+    ends = (0, n_c - 1) if n_c > 1 else ()
+    if aligned:
+        for chip in range(n_c):
+            if chip in ends:
+
+                @pl.when(z != n_c - 1 - chip)
+                def _():
+                    sibling_rows(chip)
+                    add_product(chip)
+            else:
+                sibling_rows(chip)
+                add_product(chip)
+        if n_c > 1:
+            pass_on(n_c - 1)
+        for chip in ends:
+
+            @pl.when(z == n_c - 1 - chip)
+            def _():
+                sibling_rows(chip)
+                add_product(chip)
+    else:
+        if n_c > 1:
+            pass_on(n_c - 1)
+        for chip in range(n_c):
+            sibling_rows(chip)
+
+        def whole_body(s, carry):
+            left = f_all[s].reshape(rows, width)
+            acc[s] = acc[s] + dot(left, w_all[...].reshape(width, columns))
+            return carry
+
+        lax.fori_loop(0, n_seq, whole_body, 0)
+
+    def round_body(s, carry):
+        proj_out[s] = acc[s].astype(bf16)
+        return carry
+
+    lax.fori_loop(0, n_seq, round_body, 0)
 
     for copy in pending:
         copy.wait_send()
@@ -297,16 +369,15 @@
 
                 @pl.when(here)
                 def _():
-                    @pl.when(onward)
-                    def _():
-                        copy_w(w_all.at[owner, piece], owner, piece, way, distance).wait_send()
+                    if distance < n_c - 1:
+
+                        @pl.when(onward)
+                        def _():
+                            copy_w(w_all.at[owner, piece], owner, piece, way, distance).wait_send()
 
                     share(
                         w_all, w_send, w_recv, owner, piece, way, distance, n_c, sibling
                     ).wait_send()
-
-    own_f.wait()
-    own_w.wait()
 
 
 def relay_f(peers, pair, got_f, send_f, f_all):
@@ -329,31 +400,40 @@
     )
 
 
-def gather_both(frames, weight, n_seq, n_dp):
+def gather_project(frames, weight, rate_columns, n_seq, n_dp):
     clips, slab_len, width = frames.shape
     depth, columns = weight.shape
     n_a, n_c = n_seq // 2, n_dp // 2
-    halves = frames.reshape(2, clips * slab_len // 2, width)
+    rows = clips * slab_len
+    halves = frames.reshape(2, rows // 2, width)
     pieces = weight.reshape(2, depth // 2, columns)
-    f_all, w_all = pl.pallas_call(
+    return pl.pallas_call(
         functools.partial(gather_kernel, n_seq, n_dp),
         out_shape=(
-            jax.ShapeDtypeStruct((n_seq,) + halves.shape, bf16),
-            jax.ShapeDtypeStruct((n_dp,) + pieces.shape, bf16),
+            jax.ShapeDtypeStruct((n_seq, rows, columns), bf16),
+            jax.ShapeDtypeStruct((n_seq, rows, rate_columns.shape[1]), f32),
         ),
-        in_specs=[pl.BlockSpec(memory_space=pl.ANY)] * 2,
-        out_specs=(pl.BlockSpec(memory_space=pl.ANY),) * 2,
+        in_specs=[
+            pl.BlockSpec(memory_space=pl.ANY),
+            pl.BlockSpec(memory_space=pl.ANY),
+            pl.BlockSpec(memory_space=pltpu.VMEM),
+        ],
+        out_specs=(pl.BlockSpec(memory_space=pltpu.VMEM),) * 2,
         scratch_shapes=[
+            pltpu.VMEM((n_seq,) + halves.shape, bf16),
+            pltpu.VMEM((n_dp,) + pieces.shape, bf16),
+            pltpu.VMEM((n_seq, rows, columns), f32),
             pltpu.SemaphoreType.DMA((2 * n_a + 2 * (n_a - 1),)),
             pltpu.SemaphoreType.DMA((n_seq, 2)),
             pltpu.SemaphoreType.DMA((4 * n_c * 2,)),
             pltpu.SemaphoreType.DMA((n_dp, 2)),
             pltpu.SemaphoreType.DMA((2,)),
         ],
-        compiler_params=pltpu.CompilerParams(collective_id=0, has_side_effects=True),
-        name="gather_both",
-    )(halves, pieces)
-    return f_all.reshape(n_seq * clips * slab_len, width), w_all.reshape(n_dp * depth, columns)
+        compiler_params=pltpu.CompilerParams(
+            collective_id=0, has_side_effects=True, vmem_limit_bytes=48 * 1024 * 1024
+        ),
+        name="gather_project",
+    )(halves, pieces, rate_columns)
 
 
 def exchange_kernel(n_seq, source, result, send, recv, own_sem):
@@ -447,10 +527,12 @@
     if padded > mine:
         parts = [jnp.pad(part, ((0, 0), (0, (padded - mine) * size))) for part in parts]
     weight = jnp.concatenate(parts, axis=1)
-    rows, weight = gather_both(frames, weight, length, lax.axis_size("dp"))
-    projected = jnp.dot(rows, weight, preferred_element_type=f32).astype(bf16)
+    rate_columns = jnp.pad(own(rate_weight, 1), ((0, 0), (0, 128 - padded)))
+    projected, logits = gather_project(
+        frames, weight, rate_columns, length, lax.axis_size("dp")
+    )
     projected = projected.reshape(length, clips, slab_len, groups * 3 * lanes)
-    rates = jnp.dot(rows, own(rate_weight, 1), preferred_element_type=f32)
+    rates = logits[..., :padded]
     rates = jax.nn.sigmoid(rates + own(rate_bias, 0)) / (MB * (size + inner))
     rates = rates.reshape(length, clips, batches, MB, groups, PAIR).transpose(4, 0, 2, 1, 5, 3)
     rates = rates.reshape(groups, length * batches, 1, blocks * MB)

time: 140 us -> 119 us (0.85)
  matrix products: 17 us -> 0 us
  Pallas kernels: 113 us -> 108 us
  local copies, waits for them, and re-layouts: 8.05 us -> 10.3 us
    dot_general x2 -> x0, matrix products: 17 us -> none  [the longest x1 12.4 us: on_device(): projected = jnp.dot(rows, weight, preferred_element_type=f32).astype(bf16)]
    pallas_call x1, Pallas kernels: 76.1 us -> 71.2 us  [gather_project(): pl.pallas_call(functools.partial(gather_kernel, n_seq, n_dp), out_shape=(...]
    unnamed x10 -> x13, local copies, waits for them, and re-layouts: 0.9 us -> 2.73 us
where the time goes in v4:
time: 119 us
  Pallas kernels  108 us (91%)
  local copies, waits for them, and re-layouts  10.3 us (9%)
    pallas_call x1, Pallas kernels, gather_project(): pl.pallas_call(functools.partial(gather_kernel, n_seq, n_dp), out_shape=(...  71.2 us
    pallas_call x1, Pallas kernels, on_device(): pl.pallas_call(functools.partial(ttt_kernel, groups, clips), out_shape=ja...  23.5 us
    pallas_call x1, Pallas kernels, exchange(): pl.pallas_call(functools.partial(exchange_kernel, n_seq), out_shape=jax.S...  13.2 us
    unnamed x13, local copies, waits for them, and re-layouts  2.73 us

profile of v4, /device:TPU:0, one launch (start us, length us, event | category | flops | bytes accessed | tf_op | source)
XLA Modules:
  0.0 118.5 jit_solution(8206965116992842207)
XLA Ops:
  0.0 0.0 copy-start
  0.0 1.3 %constant_dynamic-slice_fusion.8 = (bf16[384,384]{1,0:T(8,128)(2,1)S(1)}, bf16[384,384]{1,0:T(8,128)(2,1)S(1)}, bf16[384,384]{1,0:T(8,128)(2,1)S(1)}) fusion(bf16[384,4608]{1,0:T(8,128)(2,1)} %param.9, s32[]{:T(128)S(6)} %select_n.8, s32[]{:T(128)S(6)} %select_n.19, s32[]{:T(128)S(6)} %select_n.18), kind=kLoop, calls=%fused_computation.11 | loop fusion | bytes 1769484 | tf_op jit(solution)/shard_map/dynamic_slice | solution.py:524
  1.3 0.1 pad_maximum_fusion
  1.4 0.0 copy-done
  1.4 0.4 copy.23
  1.8 0.2 pad.8.r_ref
  2.0 0.0 copy-start.2
  2.0 1.4 %copy-done.2 = bf16[2,128,3072]{2,1,0:T(8,128)(2,1)S(1)} copy-done((bf16[2,128,3072]{2,1,0:T(8,128)(2,1)S(1)}, bf16[2,128,3072]{2,1,0:T(8,128)(2,1)}, u32[]{:S(2)}) %copy-start.2) | copy-done | bytes 1572888
  3.4 0.0 copy-start.4
  3.4 71.2 %gather_project.1 = (bf16[4,256,1152]{2,1,0:T(8,128)(2,1)S(1)}, f32[4,256,128]{2,1,0:T(8,128)S(1)}) custom-call(bf16[2,128,3072]{2,1,0:T(8,128)(2,1)S(1)} %copy-done.2, bf16[2,192,1152]{2,1,0:T(8,128)(2,1)S(1)} %bitcast.15, bf16[3072,128]{1,0:T(8,128)(2,1)S(1)} %pad.8.r_ref), custom_call_target="tpu_custom_call" | custom-call | tf_op jit(solution)/shard_map/gather_project/pallas_call | solution.py:410
  74.6 0.0 copy-start.3
  74.6 0.0 copy-done.4
  74.6 0.1 dynamic_slice.31
  74.7 0.1 divide_multiply_fusion
  74.8 0.2 copy.19
  75.0 0.1 reshape.43
  75.2 0.1 reshape.44.rate_ref
  75.3 1.2 %constant_dynamic-slice_fusion.4 = (f32[1,6,64,256]{3,2,1,0:T(8,128)S(1)}, f32[1,6,64,256]{3,2,1,0:T(8,128)S(1)}) fusion(f32[2,24,64,256]{3,2,1,0:T(8,128)} %param.12, s32[]{:T(128)S(6)} %add.43, s32[]{:T(128)S(6)} %select_n.20), kind=kLoop, calls=%fused_computation.7 | loop fusion | bytes 1572872 | tf_op jit(solution)/shard_map/slice | solution.py:562
  76.5 0.0 copy-done.3
  76.5 0.1 reshape.46
  76.6 0.7 constant_dynamic-slice_fusion.1
  77.3 0.1 broadcast_in_dim.30
  77.4 0.1 broadcast_in_dim.34
  77.5 0.7 constant_dynamic-slice_fusion.3
  78.2 23.5 %fast_state.1.source = bf16[4,2,128,384]{3,2,1,0:T(8,128)(2,1)S(1)} custom-call(bf16[4,2,128,1152]{3,2,1,0:T(8,128)(2,1)S(1)} %bitcast.16, f32[3,8,1,256]{3,2,1,0:T(1,128)S(1)} %reshape.44.rate_ref, f32[3,128,256]{2,1,0:T(8,128)S(1)} %bitcast.18, f32[3,8,256]{2,1,0:T(8,128)S(1)} %pad.9.b1_in, f32[3,128,256]{2,1,0:T(8,128)S(1)} %bitcast.17, ...), custom_call_target="tpu_custom_call" | custom-call | tf_op jit(solution)/shard_map/fast_state/pallas_call | solution.py:548
  101.7 0.0 copy-start.1
  101.7 0.9 copy-done.1
  102.6 13.2 %exchange.1 = bf16[4,2,128,384]{3,2,1,0:T(8,128)(2,1)} custom-call(bf16[4,2,128,384]{3,2,1,0:T(8,128)(2,1)} %copy-done.1), custom_call_target="tpu_custom_call" | custom-call | tf_op jit(solution)/shard_map/exchange/pallas_call | solution.py:477
  115.8 1.5 %copy.21 = bf16[2,128,4,384]{1,3,2,0:T(8,128)(2,1)S(1)} copy(bf16[2,128,4,384]{3,1,0,2:T(8,128)(2,1)} %bitcast.20) | data formatting | bytes 1572864 | tf_op jit(solution)/shard_map/transpose | solution.py:566
  117.3 1.2 copy.22
  (10 shorter events, 0.1 us)
Async XLA Ops:
  0.0 1.4 %copy-start = (bf16[3072,24]{0,1:T(8,128)(2,1)S(1)}, bf16[3072,24]{0,1:T(8,128)(2,1)}, u32[]{:S(2)}) copy-start(bf16[3072,24]{0,1:T(8,128)(2,1)} %param.10) | copy-start | bytes 442372
  2.0 1.4 %copy-start.2 = (bf16[2,128,3072]{2,1,0:T(8,128)(2,1)S(1)}, bf16[2,128,3072]{2,1,0:T(8,128)(2,1)}, u32[]{:S(2)}) copy-start(bf16[2,128,3072]{2,1,0:T(8,128)(2,1)} %f_ref.1) | copy-start | bytes 4718596
  3.4 71.2 %copy-start.4 = (f32[24]{0:T(128)S(1)}, f32[24]{0:T(128)}, u32[]{:S(2)}) copy-start(f32[24]{0:T(128)} %param.11) | copy-start | bytes 292
  74.6 1.9 %copy-start.3 = (f32[1536]{0:T(1024)S(1)}, f32[1536]{0:T(1024)}, u32[]{:S(2)}) copy-start(f32[1536]{0:T(1024)} %param.15) | copy-start | bytes 18436
  101.7 0.9 copy-start.1
